TPU v7x, 256 devices: a whole 4x4x8 slice. The times are simulated.
256 devices in a mesh: ctx: 8 (over y_lo, x), fsdp: 32 (over z, y_hi, core).
Axes of the slice: x: 4, y: 4 (y_hi: 2, y_lo: 2; y = y_hi * 2 + y_lo), z: 8, core: 2. Of those that a mesh axis runs over, the one named last changes fastest.
Arguments:
- signal: bfloat16 [32, 1024, 4096], P('fsdp', 'ctx'), may hold values from -6 to 6
- query: bfloat16 [32, 1024, 4096], P('fsdp', 'ctx'), may hold values from -6 to 6
- grad_out: bfloat16 [32, 1024, 4096], P('fsdp', 'ctx'), may hold values from -6 to 6
- filters: bfloat16 [256, 64], P('fsdp'), may hold values from -0.75 to 0.75
- skip_gain: bfloat16 [4096], P('fsdp'), may hold values from -1 to 1
Outputs:
- grad_query: bfloat16 [32, 1024, 4096], P('fsdp', 'ctx')
- grad_signal: bfloat16 [32, 1024, 4096], P('fsdp', 'ctx')
- grad_filters: float32 [256, 64], P('fsdp')
- grad_skip: float32 [4096], P('fsdp')
All inputs are finite; a program needn't handle non-finite values.
Results may differ from a plain program's by a relative error of at most 0.007.
Values may be sent and summed in bfloat16 or wider, within the bound.
A program may use at most 128 MiB of HBM per device.

v0:
```python
import jax
import jax.numpy as jnp
from jax import lax
from jax.sharding import PartitionSpec as P


def passed_along(value, axis, steps):
    count = lax.axis_size(axis)
    leading, last = (max(0, -steps), min(count, count - steps))
    return lax.ppermute(value, axis, [(source, source + steps) for source in range(leading, last)])


def toeplitz_pair(filters):
    group_count = filters.shape[0]
    tap_count = filters.shape[1]
    flipped = filters[:, ::-1]
    padded = jnp.concatenate(
        [
            jnp.zeros((group_count, 1), filters.dtype),
            flipped,
            jnp.zeros((group_count, tap_count), filters.dtype),
        ],
        axis=1,
    )
    tiled = jnp.tile(padded, (1, tap_count))[:, : 2 * tap_count * tap_count]
    return tiled.reshape(group_count, tap_count, 2 * tap_count)


def fold_diagonals(products):
    group_count = products.shape[0]
    tap_count = products.shape[1]
    double = products.shape[2]
    flattened = products.reshape(group_count, tap_count * double)
    flattened = jnp.concatenate(
        [flattened, jnp.zeros((group_count, tap_count), products.dtype)], axis=1
    )
    skewed = flattened.reshape(group_count, tap_count, double + 1)
    totals = jnp.sum(skewed, axis=1)
    return totals[:, tap_count:0:-1]


def slice_work(toeplitz, signal_pairs, gated_blocks):
    filtered = jnp.einsum(
        "gim,nmgc->nigc", toeplitz, signal_pairs, preferred_element_type=jnp.float32
    )
    spread = jnp.einsum(
        "gim,nigc->nmgc", toeplitz, gated_blocks, preferred_element_type=jnp.float32
    )
    products = jnp.einsum(
        "nigc,nmgc->gim", gated_blocks, signal_pairs, preferred_element_type=jnp.float32
    )
    return (filtered, spread, fold_diagonals(products))


def local(signal, query, grad_out, filters, skip_gain):
    all_filters, all_skip = (
        lax.all_gather(filters, "fsdp", axis=0, tiled=True),
        lax.all_gather(skip_gain, "fsdp", axis=0, tiled=True),
    )
    group_count = all_filters.shape[0]
    tap_count = all_filters.shape[1]
    local_signal = signal[0]
    row_count = local_signal.shape[0]
    feature_count = local_signal.shape[1]
    group_width = feature_count // group_count
    block_count = row_count // tap_count
    batch_groups = min(group_count, 64)
    before = passed_along(local_signal[row_count - tap_count + 1 :], "ctx", 1)
    grad_f = grad_out[0].astype(jnp.float32)
    gated = (grad_f * query[0].astype(jnp.float32)).astype(jnp.bfloat16)
    extended = jnp.concatenate(
        [jnp.zeros((1, feature_count), jnp.bfloat16), before, local_signal], axis=0
    )
    extended = extended.reshape(block_count + 1, tap_count, group_count, group_width)
    paired = jnp.concatenate([extended[:-1], extended[1:]], axis=1)
    gated_blocks = gated.reshape(block_count, tap_count, group_count, group_width)
    filtered_parts = []
    spread_parts = []
    filter_parts = []
    for start_group in range(0, group_count, batch_groups):
        end_group = start_group + batch_groups
        toeplitz = toeplitz_pair(all_filters[start_group:end_group])
        filtered, spread, filter_part = slice_work(
            toeplitz, paired[:, :, start_group:end_group], gated_blocks[:, :, start_group:end_group]
        )
        filtered_parts.append(filtered.reshape(row_count, -1))
        spread_parts.append(spread.reshape(block_count, 2 * tap_count, -1))
        filter_parts.append(filter_part)
    filtered = jnp.concatenate(filtered_parts, axis=1)
    spread = jnp.concatenate(spread_parts, axis=2)
    filter_part = jnp.concatenate(filter_parts, axis=0)
    incoming = passed_along(spread[0, 1:tap_count], "ctx", -1)
    from_next = jnp.concatenate([jnp.zeros((1, feature_count), jnp.float32), incoming], axis=0)
    later = jnp.concatenate([spread[1:, :tap_count], from_next[None]], axis=0)
    back = (spread[:, tap_count:] + later).reshape(row_count, feature_count)
    skip_f = all_skip.astype(jnp.float32)
    gated_f = gated.astype(jnp.float32)
    signal_f = local_signal.astype(jnp.float32)
    grad_signal = (back + skip_f * gated_f).astype(jnp.bfloat16)
    grad_query = (grad_f * (filtered + skip_f * signal_f)).astype(jnp.bfloat16)
    skip_part = jnp.sum(gated_f * signal_f, axis=0)
    average = 1.0 / (lax.axis_size("ctx") * lax.axis_size("fsdp"))
    filter_total, skip_total = lax.psum((filter_part, skip_part), ("ctx", "fsdp"))
    own_index = lax.axis_index("fsdp")
    filter_rows = filters.shape[0]
    skip_rows = skip_gain.shape[0]
    filter_mine = lax.dynamic_slice_in_dim(filter_total, own_index * filter_rows, filter_rows, 0)
    skip_mine = lax.dynamic_slice_in_dim(skip_total, own_index * skip_rows, skip_rows, 0)
    return (grad_query[None], grad_signal[None], filter_mine * average, skip_mine * average)


def solution(mesh):
    return jax.shard_map(
        local,
        mesh=mesh,
        in_specs=(
            P("fsdp", "ctx", None),
            P("fsdp", "ctx", None),
            P("fsdp", "ctx", None),
            P("fsdp", None),
            P("fsdp"),
        ),
        out_specs=(P("fsdp", "ctx", None), P("fsdp", "ctx", None), P("fsdp", None), P("fsdp")),
        check_vma=False,
    )
```

profile of v0, /device:TPU:1, one launch (start us, length us, event | category | flops | bytes accessed | tf_op | source)
XLA Modules:
  0.0 587.4 jit_solution(7168898738225075155)
XLA Ops:
  7.2 2.1 slice_bitcast_fusion.5
  9.3 4.9 collective-permute-start
  14.2 1.6 copy.57
  15.9 45.9 %all_gather.6 = bf16[256,64]{1,0:T(8,128)(2,1)S(1)} all-gather(bf16[8,64]{1,0:T(8,128)(2,1)S(1)} %copy-done.35), channel_id=1, replica_groups=mesh['ctx'=8,'fsdp'=32] {'fsdp'}, dimensions={0}, use_global_device_ids=true | all-gather | bytes 33792 | tf_op jit(solution)/shard_map/all_gather | solution.py:57
  65.1 3.3 tile.17
  70.9 1.8 convert_element_type.56
  72.7 3.6 fusion.39
  77.9 3.3 tile.19
  84.4 3.3 tile.41
  91.0 3.3 tile.43
  98.5 1.9 copy-done.2
  101.0 1.6 copy.76
  104.2 1.8 slice.89
  106.0 3.0 slice.127
  109.1 36.5 %all-gather = bf16[32,1,128]{2,1,0:T(2,128)(2,1)S(1)} all-gather(bf16[1,1,128]{2,1,0:T(2,128)(2,1)S(1)} %bitcast.145), channel_id=1, replica_groups=mesh['ctx'=8,'fsdp'=32] {'fsdp'}, dimensions={0}, use_global_device_ids=true | all-gather | bytes 8448 | tf_op jit(solution)/shard_map/all_gather | solution.py:58
  145.5 1.9 copy.61
  147.4 77.3 %psum.15 = f32[4096]{0:T(1024)S(1)} all-reduce(f32[4096]{0:T(1024)S(1)} %get-tuple-element.16), channel_id=1, replica_groups=mesh['ctx'=8,'fsdp'=32] {'ctx','fsdp'}, use_global_device_ids=true, to_apply=%region_6.0 | all-reduce | flops 4096 | bytes 32768 | tf_op jit(solution)/shard_map/psum | solution.py:103
  225.3 2.4 copy.58
  227.7 3.0 pad_maximum_fusion.2
  230.7 5.0 slice.88
  235.8 1.9 copy.60
  238.4 2.9 pad_maximum_fusion.1
  241.3 2.0 fusion.18
  243.4 2.0 fusion.21
  245.4 2.0 fusion.24
  247.4 1.7 convolution_bitcast_fusion.3
  249.2 1.6 convolution_bitcast_fusion.2
  250.8 1.6 convolution_bitcast_fusion.1
  255.2 17.9 %reshape.128 = f32[64,64,129]{2,1,0:T(8,128)} reshape(f32[64,8256]{1,0:T(8,128)} %concatenate.68) | data formatting | bytes 4227072 | tf_op jit(solution)/shard_map/reshape | solution.py:37
  273.1 2.8 reduce_sum.45
  276.0 2.8 copy.124
  280.3 7.5 %reshape.130 = f32[64,64,129]{2,1,0:T(8,128)} reshape(f32[64,8256]{1,0:T(8,128)} %concatenate.69) | data formatting | bytes 4227072 | tf_op jit(solution)/shard_map/reshape | solution.py:37
  287.9 2.8 reduce_sum.46
  290.8 2.9 copy.122
  298.0 7.5 %reshape.134 = f32[64,64,129]{2,1,0:T(8,128)} reshape(f32[64,8256]{1,0:T(8,128)} %concatenate.71) | data formatting | bytes 4227072 | tf_op jit(solution)/shard_map/reshape | solution.py:37
  305.5 2.8 reduce_sum.48
  308.4 7.7 %reshape.132 = f32[64,64,129]{2,1,0:T(8,128)} reshape(f32[64,8256]{1,0:T(8,128)} %concatenate.70) | data formatting | bytes 4227072 | tf_op jit(solution)/shard_map/reshape | solution.py:37
  316.2 2.8 reduce_sum.47
  319.8 3.0 convolution_bitcast_fusion
  326.3 2.6 concatenate.59
  330.5 2.7 concatenate.61
  335.1 220.6 %all-reduce.7.cloned.1.call-done = f32[256,64]{1,0:T(8,128)} async-done(((f32[256,64]{1,0:T(8,128)}), f32[256,64]{1,0:T(8,128)}) %all-reduce.7.cloned.1.call-update) | async-done | bytes 65552 | tf_op jit(solution)/shard_map/psum | solution.py:103
  557.0 1.9 copy.77
  561.0 4.7 slice_add_fusion
  565.7 3.8 copy.78
  569.5 3.0 copy.79
  572.5 4.0 fusion.3
  576.5 2.4 copy.81
  (140 shorter events, 43.0 us)
Async XLA Ops:
  7.2 8.8 %copy-start.35 = (bf16[8,64]{1,0:T(8,128)(2,1)S(1)}, bf16[8,64]{1,0:T(8,128)(2,1)}, u32[]{:S(2)}) copy-start(bf16[8,64]{1,0:T(8,128)(2,1)} %param.8) | copy-start | bytes 3076
  7.2 55.0 %copy-start.33 = (bf16[1,128,4096]{2,1,0:T(8,128)(2,1)S(1)}, bf16[1,128,4096]{2,1,0:T(8,128)(2,1)}, u32[]{:S(2)}) copy-start(bf16[1,128,4096]{2,1,0:T(8,128)(2,1)} %param.7) | copy-start | bytes 3145732
  7.2 548.5 %all-reduce.7.cloned.1.call-start = ((), (), s32[]{:S(2)}) async-start(), calls=%async_computation | async-start | bytes 262144 | tf_op jit(solution)/shard_map/psum | solution.py:103
  9.3 54.2 %copy-start.34 = (bf16[1,128,4096]{2,1,0:T(8,128)(2,1)S(1)}, bf16[1,128,4096]{2,1,0:T(8,128)(2,1)}, u32[]{:S(2)}) copy-start(bf16[1,128,4096]{2,1,0:T(8,128)(2,1)} %param.6) | copy-start | bytes 3145732
  9.3 216.0 %collective-permute-start = (bf16[63,4096]{1,0:T(8,128)(2,1)}, bf16[63,4096]{1,0:T(8,128)(2,1)}, u32[]{:S(2)}, u32[]{:S(2)}) collective-permute-start(bf16[63,4096]{1,0:T(8,128)(2,1)} %slice_bitcast_fusion.5), channel_id=1, source_target_pairs={{0,32},{32,64},{64,96},{96,128},{128,160},{160,192},{192,224},{1,3... | collective-permute-start | bytes 1548296 | tf_op jit(solution)/shard_map/ppermute | solution.py:10
  68.4 1.7 copy-start.13
  68.4 1.9 copy-start.29
  70.2 6.1 %copy-start.7 = (bf16[8,8,64,128]{3,2,1,0:T(8,128)(2,1)}, bf16[8,8,64,128]{3,2,1,0:T(8,128)(2,1)S(1)}, u32[]{:S(2)}) copy-start(bf16[8,8,64,128]{3,2,1,0:T(8,128)(2,1)S(1)} %copy.94) | copy-start | bytes 3145732
  70.8 5.5 copy-start.4
  76.3 1.5 copy-start.22
  81.2 1.6 copy-start.20
  82.8 1.4 copy-start.9
  87.7 1.6 copy-start.18
  89.4 1.5 copy-start.11
  94.3 1.6 copy-start.16
  95.9 1.0 copy-start.6
  95.9 1.6 copy-start.30
  95.9 1.9 copy-start.31
  96.0 2.2 copy-start.32
  98.4 1.9 copy-start.2
  102.6 454.4 %collective-permute-start.1 = (f32[63,4096]{1,0:T(8,128)}, f32[63,4096]{1,0:T(8,128)}, u32[]{:S(2)}, u32[]{:S(2)}) collective-permute-start(f32[63,4096]{1,0:T(8,128)} %copy.76), channel_id=1, source_target_pairs={{32,0},{64,32},{96,64},{128,96},{160,128},{192,160},{224,192},{33,... | collective-permute-start | bytes 3096584 | tf_op jit(solution)/shard_map/ppermute | solution.py:10
  106.0 3.1 copy-start.36
  147.4 90.3 %copy-start = (bf16[2,64,256,16]{1,3,0,2:T(8,128)(2,1)}, bf16[2,64,256,16]{1,3,0,2:T(8,128)(2,1)S(1)}, u32[]{:S(2)}) copy-start(bf16[2,64,256,16]{1,3,0,2:T(8,128)(2,1)S(1)} %copy.61) | copy-start | bytes 3145732
  235.8 1.9 copy-start.23
  238.4 2.9 copy-start.1
  238.4 2.9 copy-start.21
  241.3 2.0 copy-start.19
  243.4 2.0 copy-start.17
  245.4 2.0 copy-start.8
  247.4 1.7 copy-start.10
  249.2 1.6 copy-start.12
  290.8 3.0 copy-start.15
  319.8 3.0 copy-start.26
  322.8 2.0 copy-start.25
  324.8 4.2 copy-start.24
  329.0 4.2 copy-start.27
  558.8 2.2 copy-start.3
  569.5 3.0 copy-start.5
  569.5 3.0 copy-start.14
  576.5 2.4 copy-start.28
Sparse Core Ops, SparseCore 0:
  319.9 235.7 all-reduce.6
where the time goes:
time: 598 us; the launch traced here: 587 us
  waiting for transfers between devices  221 us (37%)
  blocking collectives  160 us (27%)
  local copies, waits for them, and re-layouts  140 us (23%)
  other arithmetic  29.1 us (5%)
  matrix products  16.3 us (3%)
  between operations  14.9 us (2%)
  starting transfers between devices  6.45 us (1%)
    psum x1, waiting for transfers between devices, local(): lax.psum((filter_part, skip_part), ('ctx', 'fsdp'))  221 us
    psum x1, blocking collectives, local(): lax.psum((filter_part, skip_part), ('ctx', 'fsdp'))  77.3 us
    all_gather x1, blocking collectives, local(): lax.all_gather(filters, 'fsdp', axis=0, tiled=True)  45.9 us
    reshape x4, local copies, waits for them, and re-layouts, fold_diagonals(): skewed = flattened.reshape(group_count, tap_count, double + 1)  40.7 us
    all_gather x1, blocking collectives, local(): lax.all_gather(skip_gain, 'fsdp', axis=0, tiled=True)  36.5 us
    unnamed x91, local copies, waits for them, and re-layouts  28 us
    another operation x8, local copies, waits for them, and re-layouts, toeplitz_pair(): tiled = jnp.tile(padded, (1, tap_count))[:, :2 * tap_count * tap_count]  13.8 us
  transfers between devices with their start and end apart: 3, of which 1 were waited for; matrix products, arithmetic and copies ran while one was open for 27% of the time, Pallas kernels for 0%

commit v1 on v0

v1 whole, which is shorter than its diff:
```python
import functools

import jax
import jax.numpy as jnp
from jax import lax
from jax.experimental import pallas as pl
from jax.experimental.pallas import tpu as pltpu
from jax.sharding import PartitionSpec as P

MESH = pl.DeviceIdType.MESH
BF16 = jnp.bfloat16
F32 = jnp.float32
ROWS = 128
TAPS = 64
LANES = 128
WIDTH = 16
PER_TILE = LANES // WIDTH


def tile_at(j):
    return pl.ds(pl.multiple_of(j * LANES, LANES), LANES)


def lane_index(shape):
    return lax.broadcasted_iota(jnp.int32, shape, len(shape) - 1)


def as_mask(condition):
    return jnp.where(condition, 1.0, 0.0).astype(BF16)


def banded(rows, first):
    bands = []
    for g in range(PER_TILE):
        base = jnp.broadcast_to(rows[g : g + 1], (TAPS, LANES))
        bands.append(pltpu.roll(base, first, 1, stride=1, stride_axis=0).astype(BF16))
    pairs = [jnp.concatenate(bands[p : p + 2], axis=1) for p in range(0, PER_TILE, 2)]
    return jnp.concatenate(pairs, axis=0)


def convolved(bands, window, even, odd):
    parity = []
    for mask in (even, odd):
        kept = window * mask
        parity.append(jnp.concatenate([kept[:ROWS], kept[TAPS : TAPS + ROWS]], axis=1))
    products = jnp.dot(bands, jnp.concatenate(parity, axis=0), preferred_element_type=F32)
    pair_of = lane_index((TAPS, LANES)) // (2 * WIDTH)
    blocks = []
    for n in range(2):
        total = products[:TAPS, n * LANES : (n + 1) * LANES]
        for p in range(1, 4):
            part = products[p * TAPS : (p + 1) * TAPS, n * LANES : (n + 1) * LANES]
            total = jnp.where(pair_of == p, part, total)
        blocks.append(total)
    return jnp.concatenate(blocks, axis=0)


def correlated(later, earlier, masks):
    count = later.shape[0] // WIDTH
    total = None
    for n in range(0, count, 2):
        left, right = [], []
        for k in (n, n + 1):
            block = later[WIDTH * k : WIDTH * (k + 1)]
            left.append(jnp.concatenate([block * mask for mask in masks], axis=0))
            right.append(earlier[WIDTH * k : WIDTH * k + LANES])
        part = lax.dot_general(
            jnp.concatenate(left, axis=1),
            jnp.concatenate(right, axis=1),
            (((1,), (1,)), ((), ())),
            preferred_element_type=F32,
        )
        total = part if total is None else total + part
    return total


def mirror(size):
    i, j = (lax.broadcasted_iota(jnp.int32, (size, size), axis) for axis in (0, 1))
    return as_mask((i // WIDTH == j // WIDTH) & (i % WIDTH + j % WIDTH == WIDTH - 1))


def mirrored(permutation, rows):
    return jnp.dot(permutation, rows, preferred_element_type=F32).astype(BF16)


def folded(products):
    rows = []
    for g in range(PER_TILE):
        block = products[WIDTH * g : WIDTH * (g + 1)]
        skewed = pltpu.roll(block, LANES - WIDTH, 1, stride=1, stride_axis=0)
        rows.append(jnp.sum(skewed, axis=0, keepdims=True))
    return jnp.concatenate(rows, axis=0)


def kernel(
    nf, nc, chunks,
    sig, qry, gout, filt, skip,
    gq_ref, gs_ref, gp_ref,
    s, q, g, gated, flipped, hs, hg, own, skips, packed, fil, rs_src, rs_dst, cx,
    load_sem, hs_send, hs_recv, hg_send, hg_recv, fil_send, fil_recv, rs_send, rs_recv, cx_send, cx_recv,
):
    c = lax.axis_index("ctx")
    me = lax.axis_index("fsdp")
    per_chunk = nf // chunks
    half = chunks // 2
    span = per_chunk * LANES

    barrier = pltpu.get_barrier_semaphore()
    for k in range(1, nc):
        pl.semaphore_signal(barrier, inc=1, device_id={"ctx": lax.rem(c + k, nc)}, device_id_type=MESH)
    for k in range(1, nf):
        pl.semaphore_signal(barrier, inc=1, device_id={"fsdp": lax.rem(me + k, nf)}, device_id_type=MESH)

    loads = [pltpu.make_async_copy(src, dst, load_sem.at[i]) for i, (src, dst) in enumerate(((sig, s), (qry, q), (gout, g)))]
    for load in loads:
        load.start()

    taps = filt[...]
    flip = as_mask(
        lax.broadcasted_iota(jnp.int32, (TAPS, TAPS), 0) + lax.broadcasted_iota(jnp.int32, (TAPS, TAPS), 1) == TAPS - 1
    )
    packed[...] = jnp.zeros_like(packed)
    packed[0:8, 0:TAPS] = taps.astype(F32)
    packed[8:16, 0:TAPS] = jnp.dot(taps, flip, preferred_element_type=F32)
    gain = skip[...].astype(F32)
    packed[0:1, TAPS:LANES] = gain[:, 0:TAPS]
    packed[1:2, TAPS:LANES] = gain[:, TAPS:LANES]
    fil[0] = packed[...].astype(BF16)

    @pl.when(c == 0)
    def _():
        hs[...] = jnp.zeros_like(hs)

    @pl.when(c == nc - 1)
    def _():
        hg[...] = jnp.zeros_like(hg)

    for load in loads:
        load.wait()

    mirror_all, mirror_halo = mirror(ROWS), mirror(TAPS)

    def gate(j, carry):
        at = tile_at(j)
        product = (g[:, at].astype(F32) * q[:, at].astype(F32)).astype(BF16)
        gated[:, at] = product
        flipped[:, at] = mirrored(mirror_all, product)
        skips[j] = jnp.sum(product.astype(F32) * s[:, at].astype(F32), axis=0, keepdims=True)
        return carry

    lax.fori_loop(0, nf, gate, 0)

    def signal_halo(k):
        at = pl.ds(pl.multiple_of(k * span, LANES), span)
        return pltpu.make_async_remote_copy(
            s.at[pl.ds(ROWS - TAPS, TAPS), at], hs.at[:, at], hs_send.at[k], hs_recv.at[k],
            device_id={"ctx": lax.rem(c + 1, nc)}, device_id_type=MESH,
        )

    def gated_halo(k):
        at = pl.ds(pl.multiple_of(k * span, LANES), span)
        return pltpu.make_async_remote_copy(
            gated.at[pl.ds(0, TAPS), at], hg.at[:, at], hg_send.at[k], hg_recv.at[k],
            device_id={"ctx": lax.rem(c + nc - 1, nc)}, device_id_type=MESH,
        )

    pl.semaphore_wait(barrier, nc - 1 + nf - 1)

    for k in range(1, nf):
        pltpu.make_async_remote_copy(
            fil.at[0], fil.at[k], fil_send, fil_recv,
            device_id={"fsdp": lax.rem(me + k, nf)}, device_id_type=MESH,
        ).start()
    for k in range(chunks):
        pl.when(c < nc - 1)(signal_halo(k).start)
        pl.when(c > 0)(gated_halo((k + half) % chunks).start)

    lane_group = lane_index((WIDTH, LANES)) // WIDTH
    masks = [as_mask(lane_group == n) for n in range(PER_TILE)]
    even = as_mask(lane_index((192, LANES)) // WIDTH % 2 == 0)
    odd = as_mask(lane_index((192, LANES)) // WIDTH % 2 == 1)

    def own_part(j, carry):
        at = tile_at(j)
        earlier = jnp.concatenate([jnp.zeros((TAPS, LANES), BF16), s[:, at], jnp.zeros((48, LANES), BF16)], axis=0)
        own[j] = correlated(flipped[:, at], earlier, masks)
        return carry

    lax.fori_loop(0, nf, own_part, 0)

    lane = lane_index((8, LANES))
    row = lax.broadcasted_iota(jnp.int32, (8, LANES), 0)

    def halo_part(j, later, earlier):
        earlier = jnp.concatenate([earlier, jnp.zeros((112, LANES), BF16)], axis=0)
        sums = folded(own[j] + correlated(later, earlier, masks))
        direct = jnp.broadcast_to(skips[j], (8, LANES))
        extra = jnp.where(row == 0, pltpu.roll(direct, TAPS, 1), jnp.where(row == 1, direct, 0.0))
        message = jnp.where(lane < TAPS, sums, extra)
        rs_src[j] = message

        @pl.when(j == me)
        def _():
            rs_dst[0] = message

        @pl.when(j != me)
        def _():
            pltpu.make_async_remote_copy(
                rs_src.at[j], rs_dst.at[lax.rem(j - me + nf, nf)], rs_send, rs_recv,
                device_id={"fsdp": j}, device_id_type=MESH,
            ).start()

    def parameters(j):
        return fil[lax.rem(me - j + nf, nf)].astype(F32)

    def gain_of(params):
        return jnp.where(lane[:1] < TAPS, pltpu.roll(params[0:1], TAPS, 1), params[1:2])

    def query_part(j):
        at = tile_at(j)
        params = parameters(j)
        window = jnp.concatenate([hs[:, at], s[:, at]], axis=0)
        filtered = convolved(banded(params[8:16], 1), window, even, odd)
        mixed = filtered + gain_of(params) * s[:, at].astype(F32)
        gq_ref[:, at] = (g[:, at].astype(F32) * mixed).astype(BF16)

    def signal_part(j):
        at = tile_at(j)
        params = parameters(j)
        window = jnp.concatenate([gated[:, at], hg[:, at]], axis=0)
        forward = jnp.where(lane < TAPS, params[0:8], 0.0)
        back = convolved(banded(forward, 0), window, even, odd)
        gs_ref[:, at] = (back + gain_of(params) * gated[:, at].astype(F32)).astype(BF16)

    def first_half(k, carry):
        pl.when(c > 0)(signal_halo(k).wait_recv)
        pl.when(c < nc - 1)(gated_halo(k + half).wait_recv)
        for i in range(per_chunk):
            j = k * per_chunk + i
            at = tile_at(j)
            halo_part(j, flipped[0:TAPS, at], hs[:, at])
            j = (k + half) * per_chunk + i
            at = tile_at(j)
            halo_part(j, mirrored(mirror_halo, hg[:, at]), s[ROWS - TAPS : ROWS, at])

        @pl.when(k == 0)
        def _():
            pltpu.make_async_copy(fil.at[pl.ds(1, nf - 1)], fil.at[pl.ds(1, nf - 1)], fil_recv).wait()

        for i in range(per_chunk):
            query_part(k * per_chunk + i)
            signal_part((k + half) * per_chunk + i)
        return carry

    lax.fori_loop(0, half, first_half, 0)

    def second_half(k, carry):
        pl.when(c > 0)(signal_halo(k + half).wait_recv)
        pl.when(c < nc - 1)(gated_halo(k).wait_recv)
        for i in range(per_chunk):
            query_part((k + half) * per_chunk + i)
            signal_part(k * per_chunk + i)
        return carry

    lax.fori_loop(0, half, second_half, 0)

    pltpu.make_async_copy(rs_dst.at[pl.ds(1, nf - 1)], rs_dst.at[pl.ds(1, nf - 1)], rs_recv).wait()
    total = rs_dst[0]
    for k in range(1, nf):
        total = total + rs_dst[k]
    cx[0] = total
    for k in range(1, nc):
        pltpu.make_async_remote_copy(
            cx.at[0], cx.at[k], cx_send, cx_recv,
            device_id={"ctx": lax.rem(c + k, nc)}, device_id_type=MESH,
        ).start()
    pltpu.make_async_copy(cx.at[pl.ds(1, nc - 1)], cx.at[pl.ds(1, nc - 1)], cx_recv).wait()
    total = cx[lax.rem(c, nc)]
    for k in range(1, nc):
        total = total + cx[lax.rem(c - k + nc, nc)]
    gp_ref[...] = total * (1.0 / (nc * nf))

    pltpu.make_async_copy(fil.at[pl.ds(1, nf - 1)], fil.at[pl.ds(1, nf - 1)], fil_send).wait()
    pltpu.make_async_copy(rs_src.at[pl.ds(1, nf - 1)], rs_src.at[pl.ds(1, nf - 1)], rs_send).wait()
    pltpu.make_async_copy(cx.at[pl.ds(1, nc - 1)], cx.at[pl.ds(1, nc - 1)], cx_send).wait()
    for k in range(chunks):
        pl.when(c < nc - 1)(signal_halo(k).wait_send)
        pl.when(c > 0)(gated_halo(k).wait_send)


def solution(mesh):
    nc, nf = mesh.shape["ctx"], mesh.shape["fsdp"]
    chunks = min(8, nf)

    def local(signal, query, grad_out, filters, skip_gain):
        features = signal.shape[2]
        whole = (ROWS, features)
        grad_query, grad_signal, params = pl.pallas_call(
            functools.partial(kernel, nf, nc, chunks),
            out_shape=(
                jax.ShapeDtypeStruct(whole, BF16),
                jax.ShapeDtypeStruct(whole, BF16),
                jax.ShapeDtypeStruct((8, LANES), F32),
            ),
            in_specs=[pl.BlockSpec(memory_space=pl.ANY)] * 3 + [pl.BlockSpec(memory_space=pltpu.VMEM)] * 2,
            out_specs=[pl.BlockSpec(memory_space=pltpu.VMEM)] * 3,
            scratch_shapes=[
                pltpu.VMEM(whole, BF16),
                pltpu.VMEM(whole, BF16),
                pltpu.VMEM(whole, BF16),
                pltpu.VMEM(whole, BF16),
                pltpu.VMEM(whole, BF16),
                pltpu.VMEM((TAPS, features), BF16),
                pltpu.VMEM((TAPS, features), BF16),
                pltpu.VMEM((nf, LANES, LANES), F32),
                pltpu.VMEM((nf, 1, LANES), F32),
                pltpu.VMEM((16, LANES), F32),
                pltpu.VMEM((nf, 16, LANES), BF16),
                pltpu.VMEM((nf, 8, LANES), F32),
                pltpu.VMEM((nf, 8, LANES), F32),
                pltpu.VMEM((nc, 8, LANES), F32),
                pltpu.SemaphoreType.DMA((3,)),
                pltpu.SemaphoreType.DMA((chunks,)),
                pltpu.SemaphoreType.DMA((chunks,)),
                pltpu.SemaphoreType.DMA((chunks,)),
                pltpu.SemaphoreType.DMA((chunks,)),
                pltpu.SemaphoreType.DMA,
                pltpu.SemaphoreType.DMA,
                pltpu.SemaphoreType.DMA,
                pltpu.SemaphoreType.DMA,
                pltpu.SemaphoreType.DMA,
                pltpu.SemaphoreType.DMA,
            ],
            compiler_params=pltpu.CompilerParams(
                collective_id=0, has_side_effects=True, vmem_limit_bytes=40 * 1024 * 1024
            ),
        )(signal[0], query[0], grad_out[0], filters, skip_gain.reshape(1, LANES))
        grad_skip = jnp.concatenate([params[0, TAPS:], params[1, TAPS:]])
        return grad_query[None], grad_signal[None], params[:, TAPS - 1 :: -1][:, :TAPS], grad_skip

    return jax.shard_map(
        local,
        mesh=mesh,
        in_specs=(
            P("fsdp", "ctx", None),
            P("fsdp", "ctx", None),
            P("fsdp", "ctx", None),
            P("fsdp", None),
            P("fsdp"),
        ),
        out_specs=(P("fsdp", "ctx", None), P("fsdp", "ctx", None), P("fsdp", None), P("fsdp")),
        check_vma=False,
    )
```

time: 598 us -> 51.4 us (0.09); the launches traced: 587 us -> 51.2 us
  waiting for transfers between devices: 221 us -> 0 us
  blocking collectives: 160 us -> 0 us
  local copies, waits for them, and re-layouts: 140 us -> 7.02 us
  Pallas kernels: 0 us -> 42.9 us
  other arithmetic: 29.1 us -> 0.59 us
  matrix products: 16.3 us -> 0 us
  between operations: 14.9 us -> 0.66 us
  starting transfers between devices: 6.45 us -> 0 us
    psum x1 -> x0, waiting for transfers between devices: 221 us -> none  [local(): lax.psum((filter_part, skip_part), ('ctx', 'fsdp'))]
    all_gather x2 -> x0, blocking collectives: 82.3 us -> none  [the longest x1 45.9 us: local(): lax.all_gather(filters, 'fsdp', axis=0, tiled=True)]
    psum x1 -> x0, blocking collectives: 77.3 us -> none  [local(): lax.psum((filter_part, skip_part), ('ctx', 'fsdp'))]
    reshape x5 -> x0, local copies, waits for them, and re-layouts: 43.8 us -> none  [the longest x4 40.7 us: fold_diagonals(): skewed = flattened.reshape(group_count, tap_count, double + 1)]
    pallas_call x0 -> x1, Pallas kernels: none -> 42.9 us  [local(): pl.pallas_call(functools.partial(kernel, nf, nc, chunks), out_shape=(jax....]
    unnamed x91 -> x12, local copies, waits for them, and re-layouts: 28 us -> 6.28 us
    slice x12 -> x0, local copies, waits for them, and re-layouts: 19.8 us -> none  [the longest x4 10.7 us: local(): paired = jnp.concatenate([extended[:-1], extended[1:]], axis=1)]
    dot_general x12 -> x0, matrix products: 16.3 us -> none  [the longest x4 7.98 us: slice_work(): jnp.einsum('gim,nmgc->nigc', toeplitz, signal_pairs, preferred_element_ty...]
  transfers between devices with their start and end apart: 3 -> 0, of which waited for: 1 -> 0; matrix products, arithmetic and copies ran while one was open for 27% -> 0% of each run, Pallas kernels for 0% -> 0%
where the time goes in v1:
time: 51.4 us; the launch traced here: 51.2 us
  Pallas kernels  42.9 us (83%)
  local copies, waits for them, and re-layouts  7.02 us (14%)
  between operations  0.66 us (1%)
  other arithmetic  0.59 us (1%)
    pallas_call x1, Pallas kernels, local(): pl.pallas_call(functools.partial(kernel, nf, nc, chunks), out_shape=(jax....  42.9 us
    unnamed x12, local copies, waits for them, and re-layouts  6.28 us

profile of v1, /device:TPU:1, one launch (start us, length us, event | category | flops | bytes accessed | tf_op | source)
XLA Modules:
  0.0 51.2 jit_solution(902664708844770109)
XLA Ops:
  0.6 0.0 copy-start.3
  0.6 0.0 copy-start.4
  0.7 0.7 %copy-done.3 = bf16[8,64]{1,0:T(8,128)(2,1)S(1)} copy-done((bf16[8,64]{1,0:T(8,128)(2,1)S(1)}, bf16[8,64]{1,0:T(8,128)(2,1)}, u32[]{:S(2)}) %copy-start.3) | copy-done | bytes 1048
  1.3 0.0 copy-done.4
  1.3 0.0 copy-start
  1.3 1.2 %copy-done = bf16[1,128,4096]{2,1,0:T(8,128)(2,1)S(1)} copy-done((bf16[1,128,4096]{2,1,0:T(8,128)(2,1)S(1)}, bf16[1,128,4096]{2,1,0:T(8,128)(2,1)}, u32[]{:S(2)}) %copy-start) | copy-done | bytes 1048600
  2.5 0.0 copy-start.1
  2.5 1.2 %copy-done.1 = bf16[1,128,4096]{2,1,0:T(8,128)(2,1)S(1)} copy-done((bf16[1,128,4096]{2,1,0:T(8,128)(2,1)S(1)}, bf16[1,128,4096]{2,1,0:T(8,128)(2,1)}, u32[]{:S(2)}) %copy-start.1) | copy-done | bytes 1048600
  3.8 0.0 copy-start.2
  3.8 1.2 %copy-done.2 = bf16[1,128,4096]{2,1,0:T(8,128)(2,1)S(1)} copy-done((bf16[1,128,4096]{2,1,0:T(8,128)(2,1)S(1)}, bf16[1,128,4096]{2,1,0:T(8,128)(2,1)}, u32[]{:S(2)}) %copy-start.2) | copy-done | bytes 1048600
  5.0 42.9 %shard_map.84 = (bf16[128,4096]{1,0:T(8,128)(2,1)S(1)}, bf16[128,4096]{1,0:T(8,128)(2,1)S(1)}, f32[8,128]{1,0:T(8,128)S(1)}) custom-call(bf16[128,4096]{1,0:T(8,128)(2,1)S(1)} %bitcast.11, bf16[128,4096]{1,0:T(8,128)(2,1)S(1)} %bitcast.12, bf16[128,4096]{1,0:T(8,128)(2,1)S(1)} %bitcast.13, bf16[8,64]{1,0:T(8,128)(2,1)S(1)} %copy-done.3, ...), custom_call_target="tpu_custom_call" | custom-call | tf_op jit(solution)/shard_map/pallas_call | solution.py:298
  47.9 0.1 slice_bitcast_fusion.1
  48.0 0.6 %pad_maximum_fusion = f32[128]{0:T(128)} fusion(f32[64]{0:T(128)S(1)} %get-tuple-element.11, f32[64]{0:T(128)S(1)} %get-tuple-element.10), kind=kLoop, calls=%fused_computation | loop fusion | flops 128 | bytes 1024 | tf_op jit(solution)/shard_map/concatenate | solution.py:338
  48.6 0.7 %rev.3 = f32[8,64]{1,0:T(8,128)} reverse(f32[8,64]{1,0:T(8,128)S(1)} %bitcast.16), dimensions={1} | reverse | bytes 4096 | tf_op jit(solution)/shard_map/rev | solution.py:339
  49.3 1.0 %copy.11 = bf16[1,128,4096]{2,1,0:T(8,128)(2,1)} copy(bf16[1,128,4096]{2,1,0:T(8,128)(2,1)S(1)} %bitcast.15) | data formatting | bytes 2097152
  50.2 1.0 %copy.12 = bf16[1,128,4096]{2,1,0:T(8,128)(2,1)} copy(bf16[1,128,4096]{2,1,0:T(8,128)(2,1)S(1)} %bitcast.14) | data formatting | bytes 2097152
Async XLA Ops:
  0.6 0.7 %copy-start.3 = (bf16[8,64]{1,0:T(8,128)(2,1)S(1)}, bf16[8,64]{1,0:T(8,128)(2,1)}, u32[]{:S(2)}) copy-start(bf16[8,64]{1,0:T(8,128)(2,1)} %filt.1) | copy-start | bytes 3076
  0.6 0.7 %copy-start.4 = (bf16[128]{0:T(256)(128)(2,1)S(1)}, bf16[128]{0:T(256)(128)(2,1)}, u32[]{:S(2)}) copy-start(bf16[128]{0:T(256)(128)(2,1)} %param.9) | copy-start | bytes 772
  1.3 1.2 %copy-start = (bf16[1,128,4096]{2,1,0:T(8,128)(2,1)S(1)}, bf16[1,128,4096]{2,1,0:T(8,128)(2,1)}, u32[]{:S(2)}) copy-start(bf16[1,128,4096]{2,1,0:T(8,128)(2,1)} %param.5) | copy-start | bytes 3145732
  2.5 1.2 %copy-start.1 = (bf16[1,128,4096]{2,1,0:T(8,128)(2,1)S(1)}, bf16[1,128,4096]{2,1,0:T(8,128)(2,1)}, u32[]{:S(2)}) copy-start(bf16[1,128,4096]{2,1,0:T(8,128)(2,1)} %param.6) | copy-start | bytes 3145732
  3.8 1.2 %copy-start.2 = (bf16[1,128,4096]{2,1,0:T(8,128)(2,1)S(1)}, bf16[1,128,4096]{2,1,0:T(8,128)(2,1)}, u32[]{:S(2)}) copy-start(bf16[1,128,4096]{2,1,0:T(8,128)(2,1)} %param.7) | copy-start | bytes 3145732

commit v2 on v1

v2 whole, which is shorter than its diff:
```python
import functools

import jax
import jax.numpy as jnp
from jax import lax
from jax.experimental import pallas as pl
from jax.experimental.pallas import tpu as pltpu
from jax.sharding import PartitionSpec as P

MESH = pl.DeviceIdType.MESH
BF16 = jnp.bfloat16
F32 = jnp.float32
ROWS = 128
TAPS = 64
LANES = 128
WIDTH = 16
PER_TILE = LANES // WIDTH
USED = pl.ds(0, 5)
QUAD = 4
WINDOW = 2


STEP = 4


def packed_rows(taps, gains):
    lane = lane_index((8, LANES))
    row = lax.broadcasted_iota(jnp.int32, (8, LANES), 0)
    beside = pltpu.roll(pltpu.roll(taps, 4, 0), TAPS, 1)
    return jnp.where(row == 4, jnp.broadcast_to(gains, (8, LANES)), jnp.where(lane < TAPS, taps, beside))


def unpacked_taps(rows):
    lane = lane_index((8, LANES))
    row = lax.broadcasted_iota(jnp.int32, (8, LANES), 0)
    beside = pltpu.roll(pltpu.roll(rows, 4, 0), TAPS, 1)
    return jnp.where(lane < TAPS, jnp.where(row < 4, rows, beside), 0.0)


def reversed_taps(taps):
    lane = lane_index((8, LANES))
    return jnp.where(lane < TAPS, jnp.take_along_axis(taps, (LANES + TAPS - 1 - lane) % LANES, axis=1), 0.0)


def in_steps(count, body):
    step = min(STEP, count)

    def run(k, carry):
        for i in range(step):
            body(k * step + i)
        return carry

    lax.fori_loop(0, count // step, run, 0)


def tile_at(j):
    return pl.ds(pl.multiple_of(j * LANES, LANES), LANES)


def lane_index(shape):
    return lax.broadcasted_iota(jnp.int32, shape, len(shape) - 1)


def as_mask(condition):
    return jnp.where(condition, 1.0, 0.0).astype(BF16)


def banded(rows, first):
    bands = []
    for g in range(PER_TILE):
        base = jnp.broadcast_to(rows[g : g + 1], (TAPS, LANES))
        bands.append(pltpu.roll(base, first, 1, stride=1, stride_axis=0).astype(BF16))
    pairs = [jnp.concatenate(bands[p : p + 2], axis=1) for p in range(0, PER_TILE, 2)]
    return jnp.concatenate(pairs, axis=0)


def convolved(bands, window, even, odd):
    parity = []
    for mask in (even, odd):
        kept = window * mask
        parity.append(jnp.concatenate([kept[:ROWS], kept[TAPS : TAPS + ROWS]], axis=1))
    products = jnp.dot(bands, jnp.concatenate(parity, axis=0), preferred_element_type=F32)
    pair_of = lane_index((TAPS, LANES)) // (2 * WIDTH)
    blocks = []
    for n in range(2):
        total = products[:TAPS, n * LANES : (n + 1) * LANES]
        for p in range(1, 4):
            part = products[p * TAPS : (p + 1) * TAPS, n * LANES : (n + 1) * LANES]
            total = jnp.where(pair_of == p, part, total)
        blocks.append(total)
    return jnp.concatenate(blocks, axis=0)


def correlated(blocks, windows, masks):
    total = None
    for n in range(0, TAPS // WIDTH, 2):
        left, right = [], []
        for k in (n, n + 1):
            block = blocks[WIDTH * k : WIDTH * (k + 1)]
            left.append(jnp.concatenate([block * mask for mask in masks], axis=0))
            right.append(windows[WIDTH * k : WIDTH * k + LANES])
        part = lax.dot_general(
            jnp.concatenate(left, axis=1),
            jnp.concatenate(right, axis=1),
            (((1,), (1,)), ((), ())),
            preferred_element_type=F32,
        )
        total = part if total is None else total + part
    return total


def mirror(size):
    i, j = (lax.broadcasted_iota(jnp.int32, (size, size), axis) for axis in (0, 1))
    return as_mask((i // WIDTH == j // WIDTH) & (i % WIDTH + j % WIDTH == WIDTH - 1))


def mirrored(permutation, rows):
    return jnp.dot(permutation, rows, preferred_element_type=F32).astype(BF16)


def folded(products, first):
    rows = []
    for g in range(PER_TILE):
        block = products[WIDTH * g : WIDTH * (g + 1)]
        skewed = pltpu.roll(block, first, 1, stride=1, stride_axis=0)
        rows.append(jnp.sum(skewed, axis=0, keepdims=True))
    return jnp.concatenate(rows, axis=0)


def kernel(
    nf, nc,
    sig, qry, gout, filt_in, skip_in,
    gq_ref, gs_ref, gp_ref,
    filt, skip, s, q, g, gated, flipped, hs, hg, own, skips, fil, rs_src, rs_dst, quad_src, quad_dst, ctx_dst,
    load_sem, hs_send, hs_recv, hg_send, hg_recv, fil_send, fil_recv, sum_send, sum_recv,
):
    c = lax.axis_index("ctx")
    me = lax.axis_index("fsdp")
    nz = nf // QUAD
    own_z, own_u = me // QUAD, lax.rem(me, QUAD)
    half = nz // 2
    span = QUAD * LANES

    def above(k):
        return {"fsdp": lax.rem(own_z + k, nz) * QUAD + own_u}

    def beside(k):
        return {"fsdp": own_z * QUAD + lax.rem(own_u + k, QUAD)}

    def along(k):
        return {"ctx": lax.rem(c + k, nc)}

    following, preceding = {"ctx": lax.rem(c + 1, nc)}, {"ctx": lax.rem(c + nc - 1, nc)}

    def send(src, dst, sends, arrivals, device):
        copy = pltpu.make_async_remote_copy(src, dst, sends, arrivals, device_id=device, device_id_type=MESH)
        copy.start()

    def await_bytes(ref, semaphore):
        pltpu.make_async_copy(ref, ref, semaphore).wait()

    peers = [along(k) for k in range(1, nc)] + [above(k) for k in range(1, nz)] + [beside(k) for k in range(1, QUAD)]
    barrier = pltpu.get_barrier_semaphore()
    for peer in peers:
        pl.semaphore_signal(barrier, inc=1, device_id=peer, device_id_type=MESH)

    loads = [pltpu.make_async_copy(src, dst, load_sem.at[i]) for i, (src, dst) in enumerate(((filt_in, filt), (skip_in, skip), (qry, q), (gout, g), (sig, s)))]
    for load in loads:
        load.start()

    for load in loads[:2]:
        load.wait()
    wide = jnp.concatenate([filt[...].astype(F32), jnp.zeros((8, LANES - TAPS), F32)], axis=1)
    fil[0, 0] = packed_rows(wide, skip[...].astype(F32))

    @pl.when(c == 0)
    def _():
        hs[...] = jnp.zeros_like(hs)

    @pl.when(c == nc - 1)
    def _():
        hg[...] = jnp.zeros_like(hg)

    lane_group = lane_index((WIDTH, LANES)) // WIDTH
    masks = [as_mask(lane_group == n) for n in range(PER_TILE)]
    even = as_mask(lane_index((192, LANES)) // WIDTH % 2 == 0)
    odd = as_mask(lane_index((192, LANES)) // WIDTH % 2 == 1)
    mirror_all = mirror(ROWS)
    nothing = jnp.zeros((48, LANES), BF16)
    middle = half * QUAD

    def gate(j):
        at = tile_at(j)
        gated[:, at] = (g[:, at].astype(F32) * q[:, at].astype(F32)).astype(BF16)

    def own_before(j):
        at = tile_at(j)
        skips[j] = jnp.sum(gated[:, at].astype(F32) * s[:, at].astype(F32), axis=0, keepdims=True)
        turned = mirrored(mirror_all, gated[:, at])
        flipped[:, at] = turned[:TAPS]
        own[j] = correlated(turned[TAPS:], jnp.concatenate([s[:, at], nothing], axis=0), masks)

    def own_after(j):
        at = tile_at(j)
        skips[j] = jnp.sum(gated[:, at].astype(F32) * s[:, at].astype(F32), axis=0, keepdims=True)
        turned = mirrored(mirror_all, s[:, at])
        flipped[:, at] = turned[TAPS:]
        own[j] = correlated(turned[:TAPS], jnp.concatenate([gated[:, at], nothing], axis=0), masks)

    def own_parts():
        in_steps(middle, own_before)
        in_steps(middle, lambda j: own_after(j + middle))

    def gate_all():
        for load in loads[2:4]:
            load.wait()
        in_steps(nf, gate)

    def signal_halo(k):
        at = pl.ds(pl.multiple_of(k * span, LANES), span)
        return pltpu.make_async_remote_copy(
            s.at[pl.ds(ROWS - TAPS, TAPS), at], hs.at[:, at], hs_send.at[k], hs_recv.at[k],
            device_id=following, device_id_type=MESH,
        )

    def gated_halo(k):
        at = pl.ds(pl.multiple_of(k * span, LANES), span)
        return pltpu.make_async_remote_copy(
            gated.at[pl.ds(0, TAPS), at], hg.at[:, at], hg_send.at[k], hg_recv.at[k],
            device_id=preceding, device_id_type=MESH,
        )

    window = min(WINDOW, nz)

    def next_halos(k):
        @pl.when(k < nz - window)
        def _():
            @pl.when(c < nc - 1)
            def _():
                signal_halo(k).wait_send()
                signal_halo(k + window).start()

            @pl.when(c > 0)
            def _():
                gated_halo(lax.rem(k + half, nz)).wait_send()
                gated_halo(lax.rem(k + window + half, nz)).start()

    early = own_z < half
    loads[4].wait()

    @pl.when(early)
    def _():
        gate_all()
        own_parts()

    pl.semaphore_wait(barrier, len(peers))

    quad_filters = fil.at[0, pl.ds(1, QUAD - 1), USED]
    far_filters = fil.at[pl.ds(1, nz - 1), pl.ds(0, QUAD), USED]
    for k in range(1, QUAD):
        send(fil.at[0, 0, USED], fil.at[0, k, USED], fil_send.at[0], fil_recv.at[0], beside(k))
    for k in range(window):
        pl.when(c < nc - 1)(signal_halo(k).start)

    pl.when(jnp.logical_not(early))(gate_all)

    for k in range(window):
        pl.when(c > 0)(gated_halo((k + half) % nz).start)

    await_bytes(quad_filters, fil_recv.at[0])
    for k in range(1, nz):
        send(
            fil.at[0, pl.ds(0, QUAD), USED], fil.at[k, pl.ds(0, QUAD), USED], fil_send.at[1], fil_recv.at[1], above(k)
        )

    pl.when(jnp.logical_not(early))(own_parts)

    def halo_before(j):
        at = tile_at(j)
        windows = jnp.concatenate([hs[:, at], s[0:112, at]], axis=0)
        sums = folded(own[j] + correlated(flipped[:, at], windows, masks), LANES - WIDTH)
        rs_src[j] = packed_rows(reversed_taps(sums), skips[j])

    def halo_after(j):
        at = tile_at(j)
        windows = jnp.concatenate([gated[TAPS:ROWS, at], hg[:, at], nothing], axis=0)
        sums = folded(own[j] + correlated(flipped[:, at], windows, masks), LANES - WIDTH + 1)
        rs_src[j] = packed_rows(sums, skips[j])

    def send_sums(z):
        @pl.when(z != own_z)
        def _():
            send(
                rs_src.at[pl.ds(z * QUAD, QUAD), USED],
                rs_dst.at[lax.rem(z - own_z + nz, nz), pl.ds(0, QUAD), USED],
                sum_send.at[0], sum_recv.at[0], {"fsdp": z * QUAD + own_u},
            )

    def parameters(j):
        return fil[lax.rem(own_z - j // QUAD + nz, nz), lax.rem(own_u - lax.rem(j, QUAD) + QUAD, QUAD)]

    def query_part(j):
        at = tile_at(j)
        params = parameters(j)
        window = jnp.concatenate([hs[:, at], s[:, at]], axis=0)
        filtered = convolved(banded(reversed_taps(unpacked_taps(params)), 1), window, even, odd)
        mixed = filtered + params[4:5] * s[:, at].astype(F32)
        gq_ref[:, at] = (g[:, at].astype(F32) * mixed).astype(BF16)

    def signal_part(j):
        at = tile_at(j)
        params = parameters(j)
        window = jnp.concatenate([gated[:, at], hg[:, at]], axis=0)
        back = convolved(banded(unpacked_taps(params), 0), window, even, odd)
        gs_ref[:, at] = (back + params[4:5] * gated[:, at].astype(F32)).astype(BF16)

    def first_half(k, carry):
        pl.when(c > 0)(signal_halo(k).wait_recv)
        pl.when(c < nc - 1)(gated_halo(k + half).wait_recv)
        next_halos(k)
        for i in range(QUAD):
            halo_before(k * QUAD + i)
            halo_after((k + half) * QUAD + i)
        send_sums(k)
        send_sums(k + half)
        return carry

    lax.fori_loop(0, half, first_half, 0)
    await_bytes(far_filters, fil_recv.at[1])

    far_sums = rs_dst.at[pl.ds(1, nz - 1), pl.ds(0, QUAD), USED]
    quad_sums = quad_dst.at[pl.ds(1, QUAD - 1), USED]
    ctx_sums = ctx_dst.at[pl.ds(1, nc - 1), USED]

    def over_z():
        await_bytes(far_sums, sum_recv.at[0])
        for i in range(QUAD):
            total = rs_src[own_z * QUAD + i, USED]
            for k in range(1, nz):
                total = total + rs_dst[k, i, USED]
            quad_src[i, USED] = total
        for k in range(1, QUAD):
            send(
                quad_src.at[lax.rem(own_u + k, QUAD), USED], quad_dst.at[k, USED],
                sum_send.at[1], sum_recv.at[1], beside(k),
            )

    def over_quad():
        await_bytes(quad_sums, sum_recv.at[1])
        total = quad_src[own_u, USED]
        for k in range(1, QUAD):
            total = total + quad_dst[k, USED]
        ctx_dst[0, USED] = total
        for k in range(1, nc):
            send(ctx_dst.at[0, USED], ctx_dst.at[k, USED], sum_send.at[2], sum_recv.at[2], along(k))

    def over_ctx():
        await_bytes(ctx_sums, sum_recv.at[2])
        total = ctx_dst[c, USED]
        for k in range(1, nc):
            total = total + ctx_dst[lax.rem(c - k + nc, nc), USED]
        gp_ref[...] = jnp.zeros_like(gp_ref)
        gp_ref[USED] = total * (1.0 / (nc * nf))

    def results(k, carry):
        next_halos(k + half)

        @pl.when(k >= half)
        def _():
            pl.when(c > 0)(signal_halo(k).wait_recv)
            pl.when(c < nc - 1)(gated_halo(k - half).wait_recv)

        for i in range(QUAD):
            query_part(k * QUAD + i)
            signal_part(lax.rem(k + half, nz) * QUAD + i)
        pl.when(k == nz - 2)(over_z)
        return carry

    lax.fori_loop(0, nz, results, 0)
    over_quad()
    over_ctx()

    await_bytes(quad_filters, fil_send.at[0])
    await_bytes(far_filters, fil_send.at[1])
    for n, sums in enumerate((far_sums, quad_sums, ctx_sums)):
        await_bytes(sums, sum_send.at[n])
    for k in range(nz - window, nz):
        pl.when(c < nc - 1)(signal_halo(k).wait_send)
        pl.when(c > 0)(gated_halo((k + half) % nz).wait_send)


def hand_over(gq_in, gs_in, params, gq_ref, gs_ref, taps_ref, gain_ref, sems):
    copies = []
    for i, (src, dst) in enumerate(((gq_in, gq_ref), (gs_in, gs_ref))):
        for n in range(2):
            rows = pl.ds(n * TAPS, TAPS)
            copies.append(pltpu.make_async_copy(src.at[rows], dst.at[rows], sems.at[i, n]))
    for copy in copies:
        copy.start()
    whole = params[...]
    taps_ref[...] = unpacked_taps(whole)[:, :TAPS]
    gain_ref[...] = whole[4:5]
    for copy in copies:
        copy.wait()


def solution(mesh):
    nc, nf = mesh.shape["ctx"], mesh.shape["fsdp"]
    nz = nf // QUAD

    def local(signal, query, grad_out, filters, skip_gain):
        features = signal.shape[2]
        whole = (ROWS, features)
        grad_query, grad_signal, params = pl.pallas_call(
            functools.partial(kernel, nf, nc),
            out_shape=(
                jax.ShapeDtypeStruct(whole, BF16),
                jax.ShapeDtypeStruct(whole, BF16),
                jax.ShapeDtypeStruct((8, LANES), F32),
            ),
            in_specs=[pl.BlockSpec(memory_space=pltpu.HBM)] * 5,
            out_specs=[pl.BlockSpec(memory_space=pltpu.VMEM)] * 3,
            scratch_shapes=[
                pltpu.VMEM((8, TAPS), BF16),
                pltpu.VMEM((1, LANES), BF16),
                pltpu.VMEM(whole, BF16),
                pltpu.VMEM(whole, BF16),
                pltpu.VMEM(whole, BF16),
                pltpu.VMEM(whole, BF16),
                pltpu.VMEM((TAPS, features), BF16),
                pltpu.VMEM((TAPS, features), BF16),
                pltpu.VMEM((TAPS, features), BF16),
                pltpu.VMEM((nf, LANES, LANES), F32),
                pltpu.VMEM((nf, 1, LANES), F32),
                pltpu.VMEM((nz, QUAD, 8, LANES), F32),
                pltpu.VMEM((nf, 8, LANES), F32),
                pltpu.VMEM((nz, QUAD, 8, LANES), F32),
                pltpu.VMEM((QUAD, 8, LANES), F32),
                pltpu.VMEM((QUAD, 8, LANES), F32),
                pltpu.VMEM((nc, 8, LANES), F32),
                pltpu.SemaphoreType.DMA((5,)),
                pltpu.SemaphoreType.DMA((nz,)),
                pltpu.SemaphoreType.DMA((nz,)),
                pltpu.SemaphoreType.DMA((nz,)),
                pltpu.SemaphoreType.DMA((nz,)),
                pltpu.SemaphoreType.DMA((2,)),
                pltpu.SemaphoreType.DMA((2,)),
                pltpu.SemaphoreType.DMA((3,)),
                pltpu.SemaphoreType.DMA((3,)),
            ],
            compiler_params=pltpu.CompilerParams(
                collective_id=0, has_side_effects=True, vmem_limit_bytes=40 * 1024 * 1024
            ),
        )(*(pltpu.with_memory_space_constraint(x, pltpu.HBM) for x in (signal[0], query[0], grad_out[0], filters, skip_gain.reshape(1, LANES))))
        grad_query, grad_signal, grad_filters, grad_skip = pl.pallas_call(
            hand_over,
            out_shape=(
                jax.ShapeDtypeStruct(whole, BF16),
                jax.ShapeDtypeStruct(whole, BF16),
                jax.ShapeDtypeStruct((8, TAPS), F32),
                jax.ShapeDtypeStruct((1, LANES), F32),
            ),
            in_specs=[pl.BlockSpec(memory_space=pltpu.VMEM)] * 3,
            out_specs=[pl.BlockSpec(memory_space=pltpu.HBM)] * 2 + [pl.BlockSpec(memory_space=pltpu.VMEM)] * 2,
            scratch_shapes=[pltpu.SemaphoreType.DMA((2, 2))],
        )(*(pltpu.with_memory_space_constraint(x, pltpu.VMEM) for x in (grad_query, grad_signal, params)))
        return grad_query[None], grad_signal[None], grad_filters, grad_skip.reshape(LANES)

    return jax.shard_map(
        local,
        mesh=mesh,
        in_specs=(
            P("fsdp", "ctx", None),
            P("fsdp", "ctx", None),
            P("fsdp", "ctx", None),
            P("fsdp", None),
            P("fsdp"),
        ),
        out_specs=(P("fsdp", "ctx", None), P("fsdp", "ctx", None), P("fsdp", None), P("fsdp")),
        check_vma=False,
    )
```

time: 51.4 us -> 37.9 us (0.74)
  local copies, waits for them, and re-layouts: 7.02 us -> 0 us
  Pallas kernels: 42.9 us -> 37.2 us
  other arithmetic: 0.59 us -> 0 us
    unnamed x12 -> x0, local copies, waits for them, and re-layouts: 6.28 us -> none
    pallas_call x1 -> x2, Pallas kernels: 42.9 us -> 37.2 us  [the longest x1 35.2 us: local(): pl.pallas_call(functools.partial(kernel, nf, nc), out_shape=(jax.ShapeDty...]
    rev x1 -> x0, local copies, waits for them, and re-layouts: 0.66 us -> none  [local(): params[:, TAPS - 1::-1][:, :TAPS]]
    concatenate x1 -> x0, other arithmetic: 0.59 us -> none  [local(): grad_skip = jnp.concatenate([params[0, TAPS:], params[1, TAPS:]])]
where the time goes in v2:
time: 37.9 us; the launch traced here: 37.8 us
  Pallas kernels  37.2 us (98%)
  between operations  0.64 us (2%)
    pallas_call x1, Pallas kernels, local(): pl.pallas_call(functools.partial(kernel, nf, nc), out_shape=(jax.ShapeDty...  35.2 us
    pallas_call x1, Pallas kernels, local(): pl.pallas_call(hand_over, out_shape=(jax.ShapeDtypeStruct(whole, BF16), j...  1.94 us

profile of v2, /device:TPU:1, one launch (start us, length us, event | category | flops | bytes accessed | tf_op | source)
XLA Modules:
  0.0 37.8 jit_solution(5192998579751666305)
XLA Ops:
  0.6 35.2 %shard_map.84 = (bf16[128,4096]{1,0:T(8,128)(2,1)S(1)}, bf16[128,4096]{1,0:T(8,128)(2,1)S(1)}, f32[8,128]{1,0:T(8,128)S(1)}) custom-call(bf16[128,4096]{1,0:T(8,128)(2,1)} %bitcast.7, bf16[128,4096]{1,0:T(8,128)(2,1)} %bitcast.8, bf16[128,4096]{1,0:T(8,128)(2,1)} %bitcast.9, bf16[8,64]{1,0:T(8,128)(2,1)} %filt_in.1, bf16[1,128]{1,0:T(2,128)(2,1)} %bitcast.10), custom_call_target="tpu_custom_call" | custom-call | tf_op jit(solution)/shard_map/pallas_call | solution.py:414
  35.9 1.9 %shard_map.85 = (bf16[128,4096]{1,0:T(8,128)(2,1)}, bf16[128,4096]{1,0:T(8,128)(2,1)}, f32[8,64]{1,0:T(8,128)}, f32[1,128]{1,0:T(1,128)}) custom-call(bf16[128,4096]{1,0:T(8,128)(2,1)S(1)} %get-tuple-element.11.gq_in, bf16[128,4096]{1,0:T(8,128)(2,1)S(1)} %get-tuple-element.12.gs_in, f32[8,128]{1,0:T(8,128)S(1)} %get-tuple-element.13.params), custom_call_target="tpu_custom_call" | custom-call | tf_op jit(solution)/shard_map/pallas_call | solution.py:455

commit v3 on v2

--- a/solution.py
+++ b/solution.py
@@ -17,7 +17,7 @@
 PER_TILE = LANES // WIDTH
 USED = pl.ds(0, 5)
 QUAD = 4
-WINDOW = 2
+WINDOW = 3
 
 
 STEP = 4
@@ -131,7 +131,7 @@
     nf, nc,
     sig, qry, gout, filt_in, skip_in,
     gq_ref, gs_ref, gp_ref,
-    filt, skip, s, q, g, gated, flipped, hs, hg, own, skips, fil, rs_src, rs_dst, quad_src, quad_dst, ctx_dst,
+    filt, skip, s, q, g, gated, flipped, hs, hg, own, skips, fil, rs_src, rs_dst, quad_src, ctx_dst,
     load_sem, hs_send, hs_recv, hg_send, hg_recv, fil_send, fil_recv, sum_send, sum_recv,
 ):
     c = lax.axis_index("ctx")
@@ -147,6 +147,9 @@
     def beside(k):
         return {"fsdp": own_z * QUAD + lax.rem(own_u + k, QUAD)}
 
+    def ring(k, i):
+        return {"ctx": lax.rem(c + k, nc), "fsdp": own_z * QUAD + lax.rem(own_u + i, QUAD)}
+
     def along(k):
         return {"ctx": lax.rem(c + k, nc)}
 
@@ -159,7 +162,7 @@
     def await_bytes(ref, semaphore):
         pltpu.make_async_copy(ref, ref, semaphore).wait()
 
-    peers = [along(k) for k in range(1, nc)] + [above(k) for k in range(1, nz)] + [beside(k) for k in range(1, QUAD)]
+    peers = [ring(k, i) for k in range(nc) for i in range(QUAD) if k + i > 0] + [above(k) for k in range(1, nz)]
     barrier = pltpu.get_barrier_semaphore()
     for peer in peers:
         pl.semaphore_signal(barrier, inc=1, device_id=peer, device_id_type=MESH)
@@ -329,8 +332,8 @@
     await_bytes(far_filters, fil_recv.at[1])
 
     far_sums = rs_dst.at[pl.ds(1, nz - 1), pl.ds(0, QUAD), USED]
-    quad_sums = quad_dst.at[pl.ds(1, QUAD - 1), USED]
-    ctx_sums = ctx_dst.at[pl.ds(1, nc - 1), USED]
+    quad_sums = ctx_dst.at[0, pl.ds(1, nc - 1), USED]
+    ctx_sums = ctx_dst.at[pl.ds(1, QUAD - 1), pl.ds(0, nc), USED]
 
     def over_z():
         await_bytes(far_sums, sum_recv.at[0])
@@ -339,26 +342,26 @@
             for k in range(1, nz):
                 total = total + rs_dst[k, i, USED]
             quad_src[i, USED] = total
-        for k in range(1, QUAD):
-            send(
-                quad_src.at[lax.rem(own_u + k, QUAD), USED], quad_dst.at[k, USED],
-                sum_send.at[1], sum_recv.at[1], beside(k),
-            )
-
-    def over_quad():
+        for i in range(QUAD):
+            owner = lax.rem(own_u + i, QUAD)
+            for k in range(nc):
+                if k + i > 0:
+                    group = min(i, 1)
+                    send(
+                        quad_src.at[owner, USED], ctx_dst.at[i, k, USED],
+                        sum_send.at[1 + group], sum_recv.at[1 + group], ring(k, i),
+                    )
+
+    def over_ctx():
         await_bytes(quad_sums, sum_recv.at[1])
-        total = quad_src[own_u, USED]
-        for k in range(1, QUAD):
-            total = total + quad_dst[k, USED]
-        ctx_dst[0, USED] = total
-        for k in range(1, nc):
-            send(ctx_dst.at[0, USED], ctx_dst.at[k, USED], sum_send.at[2], sum_recv.at[2], along(k))
-
-    def over_ctx():
         await_bytes(ctx_sums, sum_recv.at[2])
-        total = ctx_dst[c, USED]
-        for k in range(1, nc):
-            total = total + ctx_dst[lax.rem(c - k + nc, nc), USED]
+        ctx_dst[0, 0, USED] = quad_src[own_u, USED]
+        total = None
+        for k in range(nc):
+            slot = lax.rem(c - k + nc, nc)
+            for i in range(QUAD):
+                part = ctx_dst[lax.rem(own_u - i + QUAD, QUAD), slot, USED]
+                total = part if total is None else total + part
         gp_ref[...] = jnp.zeros_like(gp_ref)
         gp_ref[USED] = total * (1.0 / (nc * nf))
 
@@ -373,11 +376,10 @@
         for i in range(QUAD):
             query_part(k * QUAD + i)
             signal_part(lax.rem(k + half, nz) * QUAD + i)
-        pl.when(k == nz - 2)(over_z)
+        pl.when(k == max(nz - 6, 0))(over_z)
         return carry
 
     lax.fori_loop(0, nz, results, 0)
-    over_quad()
     over_ctx()
 
     await_bytes(quad_filters, fil_send.at[0])
@@ -436,8 +438,7 @@
                 pltpu.VMEM((nf, 8, LANES), F32),
                 pltpu.VMEM((nz, QUAD, 8, LANES), F32),
                 pltpu.VMEM((QUAD, 8, LANES), F32),
-                pltpu.VMEM((QUAD, 8, LANES), F32),
-                pltpu.VMEM((nc, 8, LANES), F32),
+                pltpu.VMEM((QUAD, nc, 8, LANES), F32),
                 pltpu.SemaphoreType.DMA((5,)),
                 pltpu.SemaphoreType.DMA((nz,)),
                 pltpu.SemaphoreType.DMA((nz,)),

time: 37.9 us -> 33.9 us (0.89)
  the two profiles are of different devices: /device:TPU:1 before, /device:TPU:97 now
where the time goes in v3:
time: 33.9 us
  Pallas kernels  33.2 us (98%)
  between operations  0.64 us (2%)
    pallas_call x1, Pallas kernels, local(): pl.pallas_call(functools.partial(kernel, nf, nc), out_shape=(jax.ShapeDty...  31.3 us
    pallas_call x1, Pallas kernels, local(): pl.pallas_call(hand_over, out_shape=(jax.ShapeDtypeStruct(whole, BF16), j...  1.94 us

profile of v3, /device:TPU:97, one launch (start us, length us, event | category | flops | bytes accessed | tf_op | source)
XLA Modules:
  0.0 33.9 jit_solution(17213453228666948581)
XLA Ops:
  0.6 31.3 %shard_map.84 = (bf16[128,4096]{1,0:T(8,128)(2,1)S(1)}, bf16[128,4096]{1,0:T(8,128)(2,1)S(1)}, f32[8,128]{1,0:T(8,128)S(1)}) custom-call(bf16[128,4096]{1,0:T(8,128)(2,1)} %bitcast.7, bf16[128,4096]{1,0:T(8,128)(2,1)} %bitcast.8, bf16[128,4096]{1,0:T(8,128)(2,1)} %bitcast.9, bf16[8,64]{1,0:T(8,128)(2,1)} %filt_in.1, bf16[1,128]{1,0:T(2,128)(2,1)} %bitcast.10), custom_call_target="tpu_custom_call" | custom-call | tf_op jit(solution)/shard_map/pallas_call | solution.py:416
  31.9 1.9 %shard_map.85 = (bf16[128,4096]{1,0:T(8,128)(2,1)}, bf16[128,4096]{1,0:T(8,128)(2,1)}, f32[8,64]{1,0:T(8,128)}, f32[1,128]{1,0:T(1,128)}) custom-call(bf16[128,4096]{1,0:T(8,128)(2,1)S(1)} %get-tuple-element.11.gq_in, bf16[128,4096]{1,0:T(8,128)(2,1)S(1)} %get-tuple-element.12.gs_in, f32[8,128]{1,0:T(8,128)S(1)} %get-tuple-element.13.params), custom_call_target="tpu_custom_call" | custom-call | tf_op jit(solution)/shard_map/pallas_call | solution.py:456

commit v4 on v3

--- a/solution.py
+++ b/solution.py
@@ -20,7 +20,7 @@
 WINDOW = 3
 
 
-STEP = 4
+STEP = 8
 
 
 def packed_rows(taps, gains):

time: 33.9 us -> 33.4 us (0.985)
  Pallas kernels: 33.2 us -> 32.6 us
    pallas_call x1, Pallas kernels: 31.3 us -> 30.7 us  [local(): pl.pallas_call(functools.partial(kernel, nf, nc), out_shape=(jax.ShapeDty...]
where the time goes in v4:
time: 33.4 us; the launch traced here: 33.3 us
  Pallas kernels  32.6 us (98%)
  between operations  0.64 us (2%)
    pallas_call x1, Pallas kernels, local(): pl.pallas_call(functools.partial(kernel, nf, nc), out_shape=(jax.ShapeDty...  30.7 us
    pallas_call x1, Pallas kernels, local(): pl.pallas_call(hand_over, out_shape=(jax.ShapeDtypeStruct(whole, BF16), j...  1.94 us

profile of v4, /device:TPU:97, one launch (start us, length us, event | category | flops | bytes accessed | tf_op | source)
XLA Modules:
  0.0 33.3 jit_solution(7832024687369134494)
XLA Ops:
  0.6 30.7 %shard_map.84 = (bf16[128,4096]{1,0:T(8,128)(2,1)S(1)}, bf16[128,4096]{1,0:T(8,128)(2,1)S(1)}, f32[8,128]{1,0:T(8,128)S(1)}) custom-call(bf16[128,4096]{1,0:T(8,128)(2,1)} %bitcast.7, bf16[128,4096]{1,0:T(8,128)(2,1)} %bitcast.8, bf16[128,4096]{1,0:T(8,128)(2,1)} %bitcast.9, bf16[8,64]{1,0:T(8,128)(2,1)} %filt_in.1, bf16[1,128]{1,0:T(2,128)(2,1)} %bitcast.10), custom_call_target="tpu_custom_call" | custom-call | tf_op jit(solution)/shard_map/pallas_call | solution.py:416
  31.3 1.9 %shard_map.85 = (bf16[128,4096]{1,0:T(8,128)(2,1)}, bf16[128,4096]{1,0:T(8,128)(2,1)}, f32[8,64]{1,0:T(8,128)}, f32[1,128]{1,0:T(1,128)}) custom-call(bf16[128,4096]{1,0:T(8,128)(2,1)S(1)} %get-tuple-element.11.gq_in, bf16[128,4096]{1,0:T(8,128)(2,1)S(1)} %get-tuple-element.12.gs_in, f32[8,128]{1,0:T(8,128)S(1)} %get-tuple-element.13.params), custom_call_target="tpu_custom_call" | custom-call | tf_op jit(solution)/shard_map/pallas_call | solution.py:456
